TPU v7x, 256 devices: a whole 4x4x8 slice. The times are simulated.
256 devices in a mesh: row: 8 (over x, core), col: 32 (over z, y).
Axes of the slice: x: 4, y: 4, z: 8, core: 2. Of those that a mesh axis runs over, the one named last changes fastest.
Arguments:
- amplitudes: bfloat16 [6144, 73728], P(('row', 'col')), may hold values from -6 to 6
- integrals: bfloat16 [1152, 73728], P('col', 'row'), may hold values from -0.0234375 to 0.0234375
- block_sizes: int32 [8], replicated, may hold values from 57 to 96, as said below
- window_irreps: int32 [2], replicated, may hold values from 0 to 7
Outputs:
- ladder: float32 [6144, 1152], P(('row', 'col'))
Inputs may be any that keep to these rules, and one draw needn't show every extreme that they name: `block_sizes`: each irrep block holds at least 57 orbitals, its first slots; at least one block is full.
All inputs are finite; a program needn't handle non-finite values.
Results may differ from a plain program's by a relative error of at most 0.0003.
Values may be sent and summed in bfloat16 or wider, within the bound.
A program may use at most 128 MiB of HBM per device.

v0:
```python
import jax
import jax.numpy as jnp
from jax import lax
from jax.sharding import PartitionSpec as P

NIRR = 8
NB = 96


def size_lookup(block_sizes, irrep_ids):
    options = jnp.arange(NIRR, dtype=jnp.int32)
    return jnp.sum(
        jnp.where(irrep_ids[:, None] == options[None, :], block_sizes[None, :], 0), axis=1
    )


def live_columns(block_sizes, pair_irrep, offset, count):
    pair_index = offset + jnp.arange(count, dtype=jnp.int32)
    irrep_c = pair_index // (NB * NB)
    slot_c = pair_index // NB % NB
    slot_d = pair_index % NB
    irrep_d = jnp.bitwise_xor(irrep_c, pair_irrep)
    live_mask = (slot_c < size_lookup(block_sizes, irrep_c)) & (
        slot_d < size_lookup(block_sizes, irrep_d)
    )
    return live_mask.astype(jnp.bfloat16)


def contract(left_rows, right_rows):
    return lax.dot_general(
        left_rows, right_rows, (((1,), (1,)), ((), ())), preferred_element_type=jnp.float32
    )


def shards(amplitudes, integrals, block_sizes, window_irreps):
    n_col = lax.axis_size("col")
    local_width = integrals.shape[1]
    window_rows = integrals.shape[0] * n_col
    transposed = lax.all_to_all(amplitudes, "row", split_axis=1, concat_axis=0, tiled=True)
    offset = lax.axis_index("row") * local_width
    live_mask = live_columns(block_sizes, window_irreps[0], offset, local_width)
    masked = transposed * live_mask[None, :]
    partial_sum = contract(masked, lax.all_gather(integrals, "col", axis=0, tiled=True))
    ladder = lax.psum_scatter(partial_sum, "row", scatter_dimension=0, tiled=True)
    size_b = jnp.sum(
        jnp.where(jnp.arange(NIRR, dtype=jnp.int32) == window_irreps[1], block_sizes, 0)
    )
    slot_mask = jnp.arange(window_rows, dtype=jnp.int32) % NB < size_b
    return jnp.where(slot_mask[None, :], ladder, jnp.float32(0.0))


def solution(mesh):
    placed = (P(("row", "col"), None), P("col", "row"), P(), P())
    return jax.shard_map(
        shards, mesh=mesh, in_specs=placed, out_specs=P(("row", "col"), None), check_vma=False
    )
```

profile of v0, /device:TPU:8, one launch (start us, length us, event | category | flops | bytes accessed | tf_op | source)
XLA Modules:
  0.0 261.7 jit_solution(1216563806489351661)
XLA Ops:
  6.5 0.0 all-gather.3.cloned.1.call-start
  6.5 0.7 all-gather.3.cloned.1.call-update
  7.3 4.0 %copy.10 = bf16[3,8,8,9216]{3,2,0,1:T(8,128)(2,1)} copy(bf16[3,8,8,9216]{3,2,1,0:T(8,128)(2,1)} %bitcast.14) | data formatting | bytes 7077888 | tf_op jit(solution)/shard_map/all_to_all | solution.py:39
  11.3 0.0 copy-start.1
  11.3 0.0 copy-start.2
  11.3 4.4 %all-to-all-start = ((bf16[24,8,9216]{2,0,1:T(8,128)(2,1)}), bf16[24,8,9216]{2,0,1:T(8,128)(2,1)S(1)}, u32[]{:S(2)}, u32[]{:S(2)}) async-start(bf16[24,8,9216]{2,0,1:T(8,128)(2,1)} %bitcast.13), calls=%async_computation | async-start | bytes 7077888 | tf_op jit(solution)/shard_map/all_to_all | solution.py:39
  15.7 0.0 reduce-scatter.4.cloned.1.call-start
  15.8 0.0 copy-done.1
  15.8 0.6 fusion.15
  16.4 0.7 add_select_fusion.1
  17.1 0.0 copy-done.2
  17.1 0.3 select_reduce_fusion
  17.4 0.7 fusion.9
  18.1 40.3 %all-to-all-done = bf16[24,8,9216]{2,0,1:T(8,128)(2,1)S(1)} async-done(((bf16[24,8,9216]{2,0,1:T(8,128)(2,1)}), bf16[24,8,9216]{2,0,1:T(8,128)(2,1)S(1)}, u32[]{:S(2)}, u32[]{:S(2)}) %all-to-all-start) | async-done | bytes 3538976 | tf_op jit(solution)/shard_map/all_to_all | solution.py:39
  58.4 2.9 %bitcast_multiply_fusion = bf16[192,9216]{1,0:T(8,128)(2,1)} fusion(bf16[24,8,9216]{2,0,1:T(8,128)(2,1)S(1)} %all-to-all-done, bf16[9216]{0:T(1024)(128)(2,1)} %fusion.9), kind=kLoop, calls=%fused_computation.1 | loop fusion | flops 1769472 | bytes 7096320 | tf_op jit(solution)/shard_map/mul | solution.py:42
  61.2 0.0 copy-start
  61.2 125.4 %all-gather.3.cloned.1.call-done = bf16[32,36,9216]{2,1,0:T(8,128)(2,1)} async-done(((bf16[1,36,9216]{2,1,0:T(8,128)(2,1)}), bf16[32,36,9216]{2,1,0:T(8,128)(2,1)}) %all-gather.3.cloned.1.call-update) | async-done | bytes 21233680 | tf_op jit(solution)/shard_map/all_gather | solution.py:43
  186.6 22.0 %reshape.60 = bf16[1152,9216]{1,0:T(8,128)(2,1)} reshape(bf16[32,36,9216]{2,1,0:T(8,128)(2,1)} %all-gather.3.cloned.1.call-done) | data formatting | bytes 42467328
  208.6 0.0 copy-done
  208.6 12.1 %fusion.16 = f32[192,1152]{1,0:T(8,128)} fusion(bf16[192,9216]{1,0:T(8,128)(2,1)S(1)} %copy-done, bf16[1152,9216]{1,0:T(8,128)(2,1)} %reshape.60), kind=kOutput, calls=%fused_computation.34 | convolution fusion | flops 4076863488 | bytes 25657344 | tf_op jit(solution)/shard_map/dot_general | solution.py:30
  220.7 0.0 reduce-scatter.4.cloned.1.call-update
  220.8 1.3 fusion.14
  222.0 0.7 fusion.10
  222.7 30.6 %reduce-scatter.4.cloned.1.call-done = f32[24,1152]{1,0:T(8,128)} async-done(((f32[192,1152]{1,0:T(8,128)}), f32[24,1152]{1,0:T(8,128)}) %reduce-scatter.4.cloned.1.call-update) | async-done | bytes 110608
  253.3 1.6 broadcast_select_fusion
Async XLA Ops:
  6.5 180.1 %all-gather.3.cloned.1.call-start = ((), (), s32[]{:S(2)}) async-start(), calls=%async_computation.2 | async-start | bytes 24330240 | tf_op jit(solution)/shard_map/all_gather | solution.py:43
  11.3 4.5 %copy-start.1 = (s32[2]{0:T(128)S(1)}, s32[2]{0:T(128)}, u32[]{:S(2)}) copy-start(s32[2]{0:T(128)} %param.7) | copy-start | bytes 28
  11.3 5.8 %copy-start.2 = (s32[8]{0:T(128)S(1)}, s32[8]{0:T(128)}, u32[]{:S(2)}) copy-start(s32[8]{0:T(128)} %param.6) | copy-start | bytes 100
  11.3 47.1 %all-to-all-start = ((bf16[24,8,9216]{2,0,1:T(8,128)(2,1)}), bf16[24,8,9216]{2,0,1:T(8,128)(2,1)S(1)}, u32[]{:S(2)}, u32[]{:S(2)}) async-start(bf16[24,8,9216]{2,0,1:T(8,128)(2,1)} %bitcast.13), calls=%async_computation | async-start | bytes 7077888 | tf_op jit(solution)/shard_map/all_to_all | solution.py:39
  15.7 237.6 %reduce-scatter.4.cloned.1.call-start = ((), (), s32[]{:S(2)}) async-start(), calls=%async_computation.3 | async-start | bytes 995328
  61.2 147.4 %copy-start = (bf16[192,9216]{1,0:T(8,128)(2,1)S(1)}, bf16[192,9216]{1,0:T(8,128)(2,1)}, u32[]{:S(2)}) copy-start(bf16[192,9216]{1,0:T(8,128)(2,1)} %bitcast_multiply_fusion) | copy-start | bytes 10616836
Sparse Core Ops, SparseCore 0:
  9.9 176.6 all-gather.2
  220.9 32.3 reduce-scatter.3
where the time goes:
time: 263 us; the launch traced here: 262 us
  waiting for transfers between devices  197 us (75%)
  local copies, waits for them, and re-layouts  26.6 us (10%)
  between operations  13.4 us (5%)
  matrix products  12.1 us (5%)
  other arithmetic  7.95 us (3%)
  starting transfers between devices  4.47 us (2%)
    all_gather x1, waiting for transfers between devices, shards(): lax.all_gather(integrals, 'col', axis=0, tiled=True)  125 us
    all_to_all x1, waiting for transfers between devices, shards(): lax.all_to_all(amplitudes, 'row', split_axis=1, concat_axis=0, tiled=True)  40.3 us
    unnamed x3, waiting for transfers between devices  31.4 us
    unnamed x7, local copies, waits for them, and re-layouts  22 us
    dot_general x1, matrix products, contract(): lax.dot_general(left_rows, right_rows, (((1,), (1,)), ((), ())), preferre...  12.1 us
  transfers between devices with their start and end apart: 3, of which 3 were waited for; matrix products, arithmetic and copies ran while one was open for 4% of the time, Pallas kernels for 0%

commit v1 on v0

--- a/solution.py
+++ b/solution.py
@@ -40,7 +40,12 @@
     offset = lax.axis_index("row") * local_width
     live_mask = live_columns(block_sizes, window_irreps[0], offset, local_width)
     masked = transposed * live_mask[None, :]
-    partial_sum = contract(masked, lax.all_gather(integrals, "col", axis=0, tiled=True))
+    partial_sum = contract(
+        masked,
+        jnp.concatenate(
+            lax.all_to_all(jnp.stack([integrals] * lax.axis_size("col")), "col", 0, 0), axis=0
+        ),
+    )
     ladder = lax.psum_scatter(partial_sum, "row", scatter_dimension=0, tiled=True)
     size_b = jnp.sum(
         jnp.where(jnp.arange(NIRR, dtype=jnp.int32) == window_irreps[1], block_sizes, 0)

time: 263 us -> 727 us (2.76)
  waiting for transfers between devices: 197 us -> 602 us
  blocking collectives: 0 us -> 47.4 us
  starting transfers between devices: 4.47 us -> 11.9 us
    all_to_all x1, waiting for transfers between devices: 40.3 us -> 557 us  [shards(): lax.all_to_all(jnp.stack([integrals] * lax.axis_size('col')), 'col', 0, 0)]
    all_gather x1 -> x0, waiting for transfers between devices: 125 us -> none  [shards(): lax.all_gather(integrals, 'col', axis=0, tiled=True)]
    all_to_all x0 -> x1, blocking collectives: none -> 47.4 us  [shards(): lax.all_to_all(amplitudes, 'row', split_axis=1, concat_axis=0, tiled=True)]
    reshape x0 -> x1, local copies, waits for them, and re-layouts: none -> 22 us  [shards(): jnp.concatenate(lax.all_to_all(jnp.stack([integrals] * lax.axis_size('col...]
    unnamed x7 -> x8, local copies, waits for them, and re-layouts: 22 us -> 0.02 us
    unnamed x3 -> x2, waiting for transfers between devices: 31.4 us -> 45 us
    another operation x0 -> x1, local copies, waits for them, and re-layouts: none -> 8.02 us  [shards(): jnp.stack([integrals] * lax.axis_size('col'))]
    all_to_all x1, starting transfers between devices: 4.43 us -> 11.9 us  [shards(): lax.all_to_all(jnp.stack([integrals] * lax.axis_size('col')), 'col', 0, 0)]
  transfers between devices with their start and end apart: 3 -> 2, of which waited for: 3 -> 2; matrix products, arithmetic and copies ran while one was open for 4% -> 1% of each run, Pallas kernels for 0% -> 0%
where the time goes in v1:
time: 727 us; the launch traced here: 726 us
  waiting for transfers between devices  602 us (83%)
  blocking collectives  47.4 us (7%)
  local copies, waits for them, and re-layouts  32.8 us (5%)
  between operations  13.5 us (2%)
  matrix products  12.1 us (2%)
  starting transfers between devices  11.9 us (2%)
    all_to_all x1, waiting for transfers between devices, shards(): lax.all_to_all(jnp.stack([integrals] * lax.axis_size('col')), 'col', 0, 0)  557 us
    all_to_all x1, blocking collectives, shards(): lax.all_to_all(amplitudes, 'row', split_axis=1, concat_axis=0, tiled=True)  47.4 us
    unnamed x2, waiting for transfers between devices  45 us
    reshape x1, local copies, waits for them, and re-layouts, shards(): jnp.concatenate(lax.all_to_all(jnp.stack([integrals] * lax.axis_size('col...  22 us
  transfers between devices with their start and end apart: 2, of which 2 were waited for; matrix products, arithmetic and copies ran while one was open for 1% of the time, Pallas kernels for 0%

profile of v1, /device:TPU:8, one launch (start us, length us, event | category | flops | bytes accessed | tf_op | source)
XLA Modules:
  0.0 726.1 jit_solution(8792312846153221937)
XLA Ops:
  6.5 2.2 copy.10
  8.8 0.0 copy-start.1
  8.8 47.4 %all_to_all.18 = bf16[24,8,9216]{2,0,1:T(8,128)(2,1)S(1)} all-to-all(bf16[24,8,9216]{2,0,1:T(8,128)(2,1)S(1)} %bitcast.12), channel_id=1, replica_groups=mesh['row'=8,'col'=32] {'row'}, dimensions={1} | all-to-all | bytes 7077888 | tf_op jit(solution)/shard_map/all_to_all | solution.py:39
  56.2 0.0 copy-done.1
  56.2 8.0 %stack.2 = bf16[32,36,9216]{2,1,0:T(8,128)(2,1)} broadcast(bf16[36,9216]{1,0:T(8,128)(2,1)S(1)} %copy-done.1), dimensions={1,2} | broadcast | bytes 21897216 | tf_op jit(solution)/shard_map/stack | solution.py:46
  64.2 0.0 copy-start.2
  64.2 0.0 copy-start.3
  64.2 11.9 %all-to-all-start.1 = ((bf16[32,36,9216]{2,1,0:T(8,128)(2,1)}), bf16[32,36,9216]{2,1,0:T(8,128)(2,1)}, u32[]{:S(2)}, u32[]{:S(2)}) async-start(bf16[32,36,9216]{2,1,0:T(8,128)(2,1)} %stack.2), calls=%async_computation.1 | async-start | bytes 47185920 | tf_op jit(solution)/shard_map/all_to_all | solution.py:46
  76.1 0.0 reduce-scatter.4.cloned.1.call-start
  76.2 0.0 copy-done.2
  76.2 0.6 fusion.15
  76.8 0.7 add_select_fusion.1
  77.4 0.0 copy-done.3
  77.4 0.3 select_reduce_fusion
  77.7 0.1 fusion.9
  77.8 2.0 broadcast_multiply_fusion
  79.8 0.0 copy-start
  79.8 556.9 %all-to-all-done.1 = bf16[32,36,9216]{2,1,0:T(8,128)(2,1)} async-done(((bf16[32,36,9216]{2,1,0:T(8,128)(2,1)}), bf16[32,36,9216]{2,1,0:T(8,128)(2,1)}, u32[]{:S(2)}, u32[]{:S(2)}) %all-to-all-start.1) | async-done | bytes 21233696 | tf_op jit(solution)/shard_map/all_to_all | solution.py:46
  636.7 22.0 %reshape.70 = bf16[1152,9216]{1,0:T(8,128)(2,1)} reshape(bf16[32,36,9216]{2,1,0:T(8,128)(2,1)} %all-to-all-done.1) | data formatting | bytes 42467328 | tf_op jit(solution)/shard_map/reshape | solution.py:45
  658.7 0.0 copy-done
  658.7 12.1 %fusion.16 = f32[192,1152]{1,0:T(8,128)} fusion(bf16[192,9216]{1,0:T(8,128)(2,1)S(1)} %bitcast.14, bf16[1152,9216]{1,0:T(8,128)(2,1)} %reshape.70), kind=kOutput, calls=%fused_computation.34 | convolution fusion | flops 4076863488 | bytes 25657344 | tf_op jit(solution)/shard_map/dot_general | solution.py:30
  670.8 0.0 reduce-scatter.4.cloned.1.call-update
  670.9 1.3 fusion.14
  672.1 0.6 fusion.10
  672.7 45.0 %reduce-scatter.4.cloned.1.call-done = f32[24,1152]{1,0:T(8,128)} async-done(((f32[192,1152]{1,0:T(8,128)}), f32[24,1152]{1,0:T(8,128)}) %reduce-scatter.4.cloned.1.call-update) | async-done | bytes 110608
  717.7 1.6 broadcast_select_fusion
Async XLA Ops:
  8.8 47.4 %copy-start.1 = (bf16[36,9216]{1,0:T(8,128)(2,1)S(1)}, bf16[36,9216]{1,0:T(8,128)(2,1)}, u32[]{:S(2)}) copy-start(bf16[36,9216]{1,0:T(8,128)(2,1)} %param.5) | copy-start | bytes 1990660
  64.2 11.9 %copy-start.2 = (s32[2]{0:T(128)S(1)}, s32[2]{0:T(128)}, u32[]{:S(2)}) copy-start(s32[2]{0:T(128)} %param.7) | copy-start | bytes 28
  64.2 13.2 %copy-start.3 = (s32[8]{0:T(128)S(1)}, s32[8]{0:T(128)}, u32[]{:S(2)}) copy-start(s32[8]{0:T(128)} %param.6) | copy-start | bytes 100
  64.2 572.5 %all-to-all-start.1 = ((bf16[32,36,9216]{2,1,0:T(8,128)(2,1)}), bf16[32,36,9216]{2,1,0:T(8,128)(2,1)}, u32[]{:S(2)}, u32[]{:S(2)}) async-start(bf16[32,36,9216]{2,1,0:T(8,128)(2,1)} %stack.2), calls=%async_computation.1 | async-start | bytes 47185920 | tf_op jit(solution)/shard_map/all_to_all | solution.py:46
  76.1 641.5 %reduce-scatter.4.cloned.1.call-start = ((), (), s32[]{:S(2)}) async-start(), calls=%async_computation.3 | async-start | bytes 995328
  79.8 578.9 %copy-start = (bf16[24,8,9216]{2,0,1:T(8,128)(2,1)S(1)}, bf16[24,8,9216]{2,0,1:T(8,128)(2,1)}, u32[]{:S(2)}) copy-start(bf16[24,8,9216]{2,0,1:T(8,128)(2,1)} %broadcast_multiply_fusion) | copy-start | bytes 10616836
Sparse Core Ops, SparseCore 0:
  671.0 46.6 reduce-scatter.3
